TPU v7x, 256 devices: a whole 4x4x8 slice. The times are simulated.
256 devices in a mesh: sec: 32 (over y, x, core), mpo: 8 (over z).
Axes of the slice: x: 4, y: 4, z: 8, core: 2. Of those that a mesh axis runs over, the one named last changes fastest.
Arguments:
- trial: bfloat16 [2, 768, 128, 128], P(None, 'sec'), may hold values from -6 to 6
- left_env: bfloat16 [24, 1024, 128, 128], P('mpo', 'sec'), may hold values from -0.5 to 0.5
- right_env: bfloat16 [24, 1024, 128, 128], P('mpo', 'sec'), may hold values from -0.109375 to 0.109375
- left_slot: int32 [768], P('sec'), may hold values from 0 to 31
- dest: int32 [768, 1], P('sec'), may hold values from 0 to 31, as said below
- right_slot: int32 [768], P('sec'), may hold values from 0 to 31
Outputs:
- applied: bfloat16 [2048, 2, 128, 128], P(('sec', 'mpo'))
Inputs may be any that keep to these rules, and one draw needn't show every extreme that they name: `dest`: on the rows of one device no destination appears more than 2 times; in every draw one destination, the same for all devices, appears exactly 2 times on every device.
All inputs are finite; a program needn't handle non-finite values.
Results may differ from a plain program's by a relative error of at most 0.017.
Values may be sent and summed in bfloat16 or wider, within the bound.
A program may use at most 128 MiB of HBM per device.

v0:
```python
import jax
import jax.numpy as jnp
from jax import lax
from jax.sharding import PartitionSpec as P


def rank_within(rows):
    width = rows.shape[-1]
    order_index = jnp.arange(width, dtype=jnp.int32)
    earlier_same = (rows[:, :, None] == rows[:, None, :]) & (
        order_index[None, None, :] < order_index[None, :, None]
    )
    return jnp.sum(earlier_same.astype(jnp.int32), axis=2)


def local(trial, left_env, right_env, left_slot, dest, right_slot):
    sec_count = lax.axis_size("sec")
    block_count = trial.shape[1]
    capacity = max(2, 2 * block_count // sec_count)
    send_slots = sec_count * capacity
    my_sec = lax.axis_index("sec")
    targets = dest[:, 0]
    all_targets, all_rights = (
        lax.all_gather(targets, "sec", axis=0, tiled=True),
        lax.all_gather(right_slot, "sec", axis=0, tiled=True),
    )
    own_ranks = rank_within(targets[None, :])[0]
    positions = targets * capacity + own_ranks
    slot_index = jnp.arange(send_slots, dtype=jnp.int32)
    block_index = jnp.arange(block_count, dtype=jnp.int32)
    slot_match = positions[None, :] == slot_index[:, None]
    slot_block = jnp.sum(jnp.where(slot_match, block_index[None, :], 0), axis=1)
    slot_live = jnp.any(slot_match, axis=1)
    target_table = all_targets.reshape(sec_count, block_count)
    right_table = all_rights.reshape(sec_count, block_count)
    table_ranks = rank_within(target_table)
    cap_index = jnp.arange(capacity, dtype=jnp.int32)
    recv_match = (target_table[:, None, :] == my_sec) & (
        table_ranks[:, None, :] == cap_index[None, :, None]
    )
    recv_right = jnp.sum(jnp.where(recv_match, right_table[:, None, :], 0), axis=2).reshape(
        send_slots
    )
    left_blocks = jnp.take(left_env, left_slot, axis=1)
    products = jnp.einsum(
        "bkij,vkjl->bvkil", left_blocks, trial, preferred_element_type=jnp.float32
    ).astype(jnp.bfloat16)
    finished = False
    outgoing = jnp.where(
        slot_live[None, None, :, None, None], jnp.take(products, slot_block, axis=2), 0
    )
    incoming = lax.all_to_all(outgoing, "sec", split_axis=2, concat_axis=2, tiled=True)
    right_blocks = jnp.take(right_env, recv_right, axis=1)
    partials = jnp.einsum(
        "bvsil,bsml->svim", incoming, right_blocks, preferred_element_type=jnp.float32
    )
    share_rows = send_slots // lax.axis_size("mpo")
    summed = lax.psum(partials.astype(jnp.bfloat16), "mpo").astype(jnp.float32)
    own_rows = lax.dynamic_slice_in_dim(summed, lax.axis_index("mpo") * share_rows, share_rows, 0)
    return own_rows.astype(jnp.bfloat16)


def solution(mesh):
    placed = (
        P(None, "sec", None, None),
        P("mpo", "sec", None, None),
        P("mpo", "sec", None, None),
        P("sec"),
        P("sec", None),
        P("sec"),
    )
    return jax.shard_map(
        local,
        mesh=mesh,
        in_specs=placed,
        out_specs=P(("sec", "mpo"), None, None, None),
        check_vma=False,
    )
```

profile of v0, /device:TPU:1, one launch (start us, length us, event | category | flops | bytes accessed | tf_op | source)
XLA Modules:
  0.0 352.8 jit_solution(9932618193276248604)
XLA Ops:
  6.5 0.8 compare_select_fusion.3
  7.3 0.8 compare_and_fusion.1
  8.2 0.9 convert_reduce_fusion.1
  9.1 1.3 dynamic-slice
  11.0 0.8 bitcast_dynamic-update-slice_fusion
  11.8 0.1 select_reduce_fusion.1
  11.9 0.1 fusion.12
  12.0 4.2 %gather_fusion = bf16[24,3,128,128]{3,2,1,0:T(8,128)(2,1)} fusion(bf16[3,32,128,128]{3,2,1,0:T(8,128)(2,1)} %param.7, s32[1024]{0:T(1024)S(1)} %pad_clamp_fusion.2), kind=kCustom, calls=%fused_computation | custom fusion | bytes 4718688 | tf_op jit(solution)/shard_map/jit(_take)/gather | solution.py:44
  16.2 5.7 %convert_bitcast_fusion = bf16[3,2,24,128,128]{4,3,2,1,0:T(8,128)(2,1)} fusion(bf16[2,24,128,128]{3,2,1,0:T(8,128)(2,1)} %param.6, bf16[24,3,128,128]{3,2,1,0:T(8,128)(2,1)} %gather_fusion, pred[24]{0:T(512)(128)(4,1)S(1)} %compare_and_fusion.1), kind=kOutput, calls=%fused_computation.11 | convolution fusion | flops 607518720 | bytes 8650776 | tf_op jit(solution)/shard_map/bkij,vkjl->bvkil/dot_general | solution.py:45
  21.9 9.4 %gather_fusion.1 = bf16[64,3,2,128,128]{4,3,2,1,0:T(8,128)(2,1)} fusion(bf16[3,2,24,128,128]{4,3,2,1,0:T(8,128)(2,1)} %convert_bitcast_fusion, s32[1024]{0:T(1024)S(1)} %pad_clamp_fusion.1), kind=kCustom, calls=%fused_computation.1 | custom fusion | bytes 25166080 | tf_op jit(solution)/shard_map/jit(_take)/gather | solution.py:50
  31.3 11.2 %fusion.1 = bf16[3,2,64,128,128]{4,3,0,1,2:T(8,128)(2,1)} fusion(bf16[64,3,2,128,128]{4,3,2,1,0:T(8,128)(2,1)} %gather_fusion.1, pred[64]{0:T(512)(128)(4,1)S(1)} %fusion.12, pred[64]{0:T(512)(128)(4,1)S(1)} %compare_and_fusion.2), kind=kLoop, calls=%fused_computation.5 | loop fusion | flops 12582912 | bytes 25165952 | tf_op jit(solution)/shard_map/jit(_where)/select_n | solution.py:49
  42.5 8.7 %all-to-all-start = ((bf16[3,2,64,128,128]{4,3,0,1,2:T(8,128)(2,1)}), bf16[3,2,64,128,128]{4,3,0,1,2:T(8,128)(2,1)}, u32[]{:S(2)}, u32[]{:S(2)}) async-start(bf16[3,2,64,128,128]{4,3,0,1,2:T(8,128)(2,1)} %fusion.1), calls=%async_computation | async-start | bytes 25165824 | tf_op jit(solution)/shard_map/all_to_all | solution.py:52
  51.3 0.2 dynamic-update-slice.1
  51.5 163.9 %all-reduce.2 = (s32[768]{0:T(1024)S(1)}, s32[768]{0:T(1024)S(1)}) all-reduce(s32[768]{0:T(1024)S(1)} %dynamic-update-slice.1, s32[768]{0:T(1024)S(1)} %get-tuple-element.7), channel_id=1, replica_groups=mesh['sec'=32,'mpo'=8] {'sec'}, use_global_device_ids=true, to_apply=%add.1 | all-reduce | flops 1536 | bytes 12288
  215.6 0.1 broadcast_in_dim_reshape.2
  215.8 0.1 copy.10
  215.9 0.2 convert_reduce_fusion
  216.1 0.1 copy.14
  216.2 0.1 reshape.181
  216.3 0.1 reshape.180
  216.4 4.1 %gather_fusion.2 = bf16[64,3,128,128]{3,2,1,0:T(8,128)(2,1)} fusion(bf16[3,32,128,128]{3,2,1,0:T(8,128)(2,1)S(1)} %copy-done, s32[1024]{0:T(1024)S(1)} %pad_clamp_fusion), kind=kCustom, calls=%fused_computation.2 | custom fusion | bytes 12583168 | tf_op jit(solution)/shard_map/jit(_take)/gather | solution.py:53
  220.5 11.8 %bitcast_convert_fusion = bf16[64,2,128,128]{3,2,1,0:T(8,128)(2,1)} fusion(bf16[3,2,64,128,128]{4,3,0,1,2:T(8,128)(2,1)} %all-to-all-done, bf16[64,3,128,128]{3,2,1,0:T(8,128)(2,1)} %gather_fusion.2, pred[64]{0:T(512)(128)(4,1)S(1)} %compare_and_fusion), kind=kOutput, calls=%fused_computation.6 | convolution fusion | flops 1615855616 | bytes 23068736 | tf_op jit(solution)/shard_map/bvsil,bsml->svim/dot_general | solution.py:54
  232.4 111.7 %all-reduce.5.cloned.1.call-done = bf16[64,2,128,128]{3,2,1,0:T(8,128)(2,1)} async-done(((bf16[64,2,128,128]{3,2,1,0:T(8,128)(2,1)}), bf16[64,2,128,128]{3,2,1,0:T(8,128)(2,1)}) %all-reduce.5.cloned.1.call-update) | async-done | bytes 4194320 | tf_op jit(solution)/shard_map/psum | solution.py:58
  344.1 1.9 convert_convert_fusion
  (22 shorter events, 0.4 us)
Async XLA Ops:
  6.5 209.9 %copy-start = (bf16[3,32,128,128]{3,2,1,0:T(8,128)(2,1)S(1)}, bf16[3,32,128,128]{3,2,1,0:T(8,128)(2,1)}, u32[]{:S(2)}) copy-start(bf16[3,32,128,128]{3,2,1,0:T(8,128)(2,1)} %param.8) | copy-start | bytes 9437188
  42.5 8.8 %copy-start.1 = (s32[24]{0:T(128)S(1)}, s32[24]{0:T(128)}, u32[]{:S(2)}) copy-start(s32[24]{0:T(128)} %param.11) | copy-start | bytes 292
  42.5 178.0 %all-to-all-start = ((bf16[3,2,64,128,128]{4,3,0,1,2:T(8,128)(2,1)}), bf16[3,2,64,128,128]{4,3,0,1,2:T(8,128)(2,1)}, u32[]{:S(2)}, u32[]{:S(2)}) async-start(bf16[3,2,64,128,128]{4,3,0,1,2:T(8,128)(2,1)} %fusion.1), calls=%async_computation | async-start | bytes 25165824 | tf_op jit(solution)/shard_map/all_to_all | solution.py:52
  51.2 292.9 %all-reduce.5.cloned.1.call-start = ((), (), s32[]{:S(2)}) async-start(), calls=%async_computation.1 | async-start | bytes 8388608 | tf_op jit(solution)/shard_map/psum | solution.py:58
Sparse Core Ops, SparseCore 0:
  232.5 111.5 all-reduce.4
where the time goes:
time: 353 us
  blocking collectives  164 us (46%)
  waiting for transfers between devices  112 us (32%)
  local copies, waits for them, and re-layouts  19.9 us (6%)
  matrix products  17.5 us (5%)
  other arithmetic  16.8 us (5%)
  between operations  14.2 us (4%)
  starting transfers between devices  8.78 us (2%)
    unnamed x1, blocking collectives  164 us
    psum x1, waiting for transfers between devices, local(): summed = lax.psum(partials.astype(jnp.bfloat16), 'mpo').astype(jnp.float32)  112 us
    dot_general x1, matrix products, local(): jnp.einsum('bvsil,bsml->svim', incoming, right_blocks, preferred_element_...  11.8 us
    select_n x1, other arithmetic, local(): jnp.where(slot_live[None, None, :, None, None], jnp.take(products, slot_b...  11.2 us
    gather x1, local copies, waits for them, and re-layouts, local(): jnp.take(products, slot_block, axis=2)  9.42 us
    all_to_all x1, starting transfers between devices, local(): lax.all_to_all(outgoing, 'sec', split_axis=2, concat_axis=2, tiled=True)  8.74 us
  transfers between devices with their start and end apart: 2, of which 1 were waited for; matrix products, arithmetic and copies ran while one was open for 1% of the time, Pallas kernels for 0%

commit v1 on v0

v1 whole, which is shorter than its diff:
```python
import jax
import jax.numpy as jnp
from jax import lax
from jax.sharding import PartitionSpec as P


def rank_within(rows):
    width = rows.shape[-1]
    order_index = jnp.arange(width, dtype=jnp.int32)
    earlier_same = (rows[:, :, None] == rows[:, None, :]) & (
        order_index[None, None, :] < order_index[None, :, None]
    )
    return jnp.sum(earlier_same.astype(jnp.int32), axis=2)


def local(trial, left_env, right_env, left_slot, dest, right_slot):
    sec_count = lax.axis_size("sec")
    block_count = trial.shape[1]
    capacity = max(2, 2 * block_count // sec_count)
    slots = sec_count * capacity
    my_sec = lax.axis_index("sec")
    targets = dest[:, 0]
    table = lax.all_gather(jnp.stack([targets, right_slot]), "sec", axis=0, tiled=False)
    target_table, right_table = table[:, 0], table[:, 1]
    table_ranks = rank_within(target_table)
    cap_index = jnp.arange(capacity, dtype=jnp.int32)
    recv_match = (target_table[:, None, :] == my_sec) & (
        table_ranks[:, None, :] == cap_index[None, :, None]
    )
    asked = jnp.sum(jnp.where(recv_match, right_table[:, None, :], 0), axis=2).reshape(slots)
    own_ranks = rank_within(targets[None, :])[0]
    positions = targets * capacity + own_ranks
    slot_match = positions[None, :] == jnp.arange(slots, dtype=jnp.int32)[:, None]
    slot_block = jnp.sum(
        jnp.where(slot_match, jnp.arange(block_count, dtype=jnp.int32)[None, :], 0), axis=1
    )
    slot_live = jnp.any(slot_match, axis=1)
    outgoing = jnp.take(right_env, asked, axis=1)
    incoming = lax.all_to_all(outgoing, "sec", split_axis=1, concat_axis=1, tiled=True)
    left_blocks = jnp.take(left_env, left_slot, axis=1)
    products = jnp.einsum(
        "bkij,vkjl->bvkil", left_blocks, trial, preferred_element_type=jnp.float32
    ).astype(jnp.bfloat16)
    right_blocks = jnp.take(incoming, positions, axis=1)
    partials = jnp.einsum(
        "bvkil,bkml->kvim", products, right_blocks, preferred_element_type=jnp.float32
    ).astype(jnp.bfloat16)
    summed = lax.psum_scatter(partials, "mpo", scatter_dimension=2, tiled=True)
    placed = jnp.where(
        slot_live[:, None, None, None], jnp.take(summed, slot_block, axis=0), 0
    )
    placed = lax.all_to_all(placed, "sec", split_axis=0, concat_axis=0, tiled=True)
    return lax.all_to_all(placed, "mpo", split_axis=0, concat_axis=2, tiled=True)


def solution(mesh):
    placed = (
        P(None, "sec", None, None),
        P("mpo", "sec", None, None),
        P("mpo", "sec", None, None),
        P("sec"),
        P("sec", None),
        P("sec"),
    )
    return jax.shard_map(
        local,
        mesh=mesh,
        in_specs=placed,
        out_specs=P(("sec", "mpo"), None, None, None),
        check_vma=False,
    )
```

time: 353 us -> 228 us (0.65)
  blocking collectives: 164 us -> 69.1 us
  matrix products: 17.5 us -> 6.74 us
  other arithmetic: 16.8 us -> 8.82 us
  waiting for transfers between devices: 112 us -> 108 us
  starting transfers between devices: 8.78 us -> 5.13 us
    unnamed x1 -> x0, blocking collectives: 164 us -> none
    psum x1 -> x0, waiting for transfers between devices: 112 us -> none  [local(): summed = lax.psum(partials.astype(jnp.bfloat16), 'mpo').astype(jnp.float32)]
    all_to_all x1, waiting for transfers between devices: 0.01 us -> 68.4 us  [local(): lax.all_to_all(outgoing, 'sec', split_axis=1, concat_axis=1, tiled=True)]
    all_to_all x0 -> x2, blocking collectives: none -> 43.2 us  [the longest x1 22.9 us: local(): lax.all_to_all(placed, 'sec', split_axis=0, concat_axis=0, tiled=True)]
    reduce_scatter x0 -> x1, waiting for transfers between devices: none -> 39.2 us  [local(): summed = lax.psum_scatter(partials, 'mpo', scatter_dimension=2, tiled=True)]
    all_gather x0 -> x1, blocking collectives: none -> 25.9 us  [local(): lax.all_gather(jnp.stack([targets, right_slot]), 'sec', axis=0, tiled=False)]
    dot_general x2 -> x1, matrix products: 17.5 us -> 6.74 us  [local(): jnp.einsum('bvkil,bkml->kvim', products, right_blocks, preferred_element_...]
    select_n x3 -> x4, other arithmetic: 11.2 us -> 7.36 us  [the longest x2 6.11 us: local(): outgoing = jnp.take(right_env, asked, axis=1)]
  transfers between devices with their start and end apart: 2 -> 2, of which waited for: 1 -> 2; matrix products, arithmetic and copies ran while one was open for 1% -> 2% of each run, Pallas kernels for 0% -> 0%
where the time goes in v1:
time: 228 us
  waiting for transfers between devices  108 us (47%)
  blocking collectives  69.1 us (30%)
  local copies, waits for them, and re-layouts  17.1 us (8%)
  between operations  13.5 us (6%)
  other arithmetic  8.82 us (4%)
  matrix products  6.74 us (3%)
  starting transfers between devices  5.13 us (2%)
    all_to_all x1, waiting for transfers between devices, local(): lax.all_to_all(outgoing, 'sec', split_axis=1, concat_axis=1, tiled=True)  68.4 us
    reduce_scatter x1, waiting for transfers between devices, local(): summed = lax.psum_scatter(partials, 'mpo', scatter_dimension=2, tiled=True)  39.2 us
    all_gather x1, blocking collectives, local(): lax.all_gather(jnp.stack([targets, right_slot]), 'sec', axis=0, tiled=False)  25.9 us
    all_to_all x1, blocking collectives, local(): lax.all_to_all(placed, 'sec', split_axis=0, concat_axis=0, tiled=True)  22.9 us
    all_to_all x1, blocking collectives, local(): lax.all_to_all(placed, 'mpo', split_axis=0, concat_axis=2, tiled=True)  20.3 us
    dot_general x1, matrix products, local(): jnp.einsum('bvkil,bkml->kvim', products, right_blocks, preferred_element_...  6.74 us
    select_n x2, other arithmetic, local(): outgoing = jnp.take(right_env, asked, axis=1)  6.11 us
    gather x1, local copies, waits for them, and re-layouts, local(): right_blocks = jnp.take(incoming, positions, axis=1)  5.13 us
  transfers between devices with their start and end apart: 2, of which 2 were waited for; matrix products, arithmetic and copies ran while one was open for 2% of the time, Pallas kernels for 0%

profile of v1, /device:TPU:1, one launch (start us, length us, event | category | flops | bytes accessed | tf_op | source)
XLA Modules:
  0.0 228.0 jit_solution(8257870481157800290)
XLA Ops:
  6.5 0.8 add_bitcast_fusion
  7.4 25.9 %all-gather.1 = s32[32,2,24]{2,1,0:T(2,128)S(1)} all-gather(s32[1,2,24]{2,1,0:T(2,128)S(1)} %add_bitcast_fusion), channel_id=2, replica_groups=mesh['sec'=32,'mpo'=8] {'sec'}, dimensions={0}, use_global_device_ids=true | all-gather | bytes 6336 | tf_op jit(solution)/shard_map/all_gather | solution.py:23
  33.3 0.1 copy.29
  33.4 0.1 copy.19
  33.4 0.2 convert_reduce_fusion
  33.6 0.1 copy.20
  33.7 0.1 reshape.180
  33.8 0.1 reshape.179
  34.0 4.0 %gather_fusion.1 = bf16[64,3,128,128]{3,2,1,0:T(8,128)(2,1)} fusion(bf16[3,32,128,128]{3,2,1,0:T(8,128)(2,1)S(1)} %copy-done, s32[1024]{0:T(1024)S(1)} %pad_clamp_fusion.2), kind=kCustom, calls=%fused_computation.1 | custom fusion | bytes 12583168 | tf_op jit(solution)/shard_map/jit(_take)/gather | solution.py:38
  38.0 6.1 %select_bitcast_fusion = bf16[3,64,128,128]{3,2,0,1:T(8,128)(2,1)} fusion(bf16[64,3,128,128]{3,2,1,0:T(8,128)(2,1)} %gather_fusion.1, pred[64]{0:T(512)(128)(4,1)S(1)} %compare_and_fusion), kind=kLoop, calls=%fused_computation.4 | loop fusion | flops 3145728 | bytes 12582976 | tf_op jit(solution)/shard_map/jit(_take)/select_n | solution.py:38
  44.1 5.1 %all-to-all-start = ((bf16[3,64,128,128]{3,2,0,1:T(8,128)(2,1)}), bf16[3,64,128,128]{3,2,0,1:T(8,128)(2,1)}, u32[]{:S(2)}, u32[]{:S(2)}) async-start(bf16[3,64,128,128]{3,2,0,1:T(8,128)(2,1)} %select_bitcast_fusion), calls=%async_computation | async-start | bytes 12582912 | tf_op jit(solution)/shard_map/all_to_all | solution.py:39
  49.3 4.3 %gather_fusion = bf16[24,3,128,128]{3,2,1,0:T(8,128)(2,1)} fusion(bf16[3,32,128,128]{3,2,1,0:T(8,128)(2,1)} %param.7, s32[1024]{0:T(1024)S(1)} %pad_clamp_fusion.3), kind=kCustom, calls=%fused_computation | custom fusion | bytes 4718688 | tf_op jit(solution)/shard_map/jit(_take)/gather | solution.py:40
  53.6 0.2 convert_reduce_fusion.1
  53.8 68.4 %all-to-all-done = bf16[3,64,128,128]{3,2,0,1:T(8,128)(2,1)} async-done(((bf16[3,64,128,128]{3,2,0,1:T(8,128)(2,1)}), bf16[3,64,128,128]{3,2,0,1:T(8,128)(2,1)}, u32[]{:S(2)}, u32[]{:S(2)}) %all-to-all-start) | async-done | bytes 6291488 | tf_op jit(solution)/shard_map/all_to_all | solution.py:39
  122.2 5.1 %gather_fusion.2 = bf16[24,3,128,128]{3,2,1,0:T(8,128)(2,1)} fusion(bf16[3,64,128,128]{3,2,0,1:T(8,128)(2,1)} %all-to-all-done, s32[1024]{0:T(1024)S(1)} %pad_clamp_fusion.1), kind=kCustom, calls=%fused_computation.2 | custom fusion | bytes 4718688 | tf_op jit(solution)/shard_map/jit(_take)/gather | solution.py:44
  127.3 6.7 %bitcast_convert_fusion = bf16[24,2,128,128]{3,2,1,0:T(8,128)(2,1)} fusion(bf16[24,3,128,128]{3,2,1,0:T(8,128)(2,1)} %gather_fusion.2, pred[24]{0:T(512)(128)(4,1)S(1)} %get-tuple-element.5, bf16[24,3,128,128]{3,2,1,0:T(8,128)(2,1)} %gather_fusion, pred[24]{0:T(512)(128)(4,1)S(1)} %compare_and_fusion.1, bf16[2,24,128,128]{3,2,1,0:T(8,128)(2,1)} %param.6), kind=kOutput, calls=%fused_computation.9 | convolution fusion | flops 1213464576 | bytes 7864368 | tf_op jit(solution)/shard_map/bvkil,bkml->kvim/dot_general | solution.py:45
  134.1 0.1 select_reduce_fusion.1
  134.2 0.1 fusion.25
  134.3 39.2 %reduce-scatter.2.cloned.1.call-done = bf16[24,2,16,128]{3,2,1,0:T(8,128)(2,1)} async-done(((bf16[24,2,128,128]{3,2,1,0:T(8,128)(2,1)}), bf16[24,2,16,128]{3,2,1,0:T(8,128)(2,1)}) %reduce-scatter.2.cloned.1.call-update) | async-done | bytes 196624 | tf_op jit(solution)/shard_map/reduce_scatter | solution.py:48
  173.5 2.3 %gather_fusion.3 = bf16[64,2,16,128]{3,2,1,0:T(8,128)(2,1)} fusion(bf16[24,2,16,128]{3,2,1,0:T(8,128)(2,1)} %reduce-scatter.2.cloned.1.call-done, s32[1024]{0:T(1024)S(1)} %pad_clamp_fusion), kind=kCustom, calls=%fused_computation.3 | custom fusion | bytes 1048832 | tf_op jit(solution)/shard_map/jit(_take)/gather | solution.py:50
  175.8 1.2 select_select_fusion
  177.1 22.9 %all_to_all.28 = bf16[64,2,16,128]{3,2,1,0:T(8,128)(2,1)S(1)} all-to-all(bf16[64,2,16,128]{3,2,1,0:T(8,128)(2,1)S(1)} %select_select_fusion), channel_id=1, replica_groups=mesh['sec'=32,'mpo'=8] {'sec'}, dimensions={0} | all-to-all | bytes 1048576 | tf_op jit(solution)/shard_map/all_to_all | solution.py:52
  200.0 20.3 %all_to_all.29 = bf16[64,2,16,128]{3,2,1,0:T(8,128)(2,1)S(1)} all-to-all(bf16[64,2,16,128]{3,2,1,0:T(8,128)(2,1)S(1)} %all_to_all.28), channel_id=1, replica_groups=mesh['sec'=32,'mpo'=8] {'mpo'}, dimensions={0} | all-to-all | bytes 1048576 | tf_op jit(solution)/shard_map/all_to_all | solution.py:53
  220.3 0.8 copy.22
  (24 shorter events, 0.2 us)
Async XLA Ops:
  6.5 27.5 %copy-start = (bf16[3,32,128,128]{3,2,1,0:T(8,128)(2,1)S(1)}, bf16[3,32,128,128]{3,2,1,0:T(8,128)(2,1)}, u32[]{:S(2)}) copy-start(bf16[3,32,128,128]{3,2,1,0:T(8,128)(2,1)} %param.8) | copy-start | bytes 9437188
  44.1 5.1 %copy-start.2 = (s32[24]{0:T(128)S(1)}, s32[24]{0:T(128)}, u32[]{:S(2)}) copy-start(s32[24]{0:T(128)} %param.9) | copy-start | bytes 292
  44.1 78.0 %all-to-all-start = ((bf16[3,64,128,128]{3,2,0,1:T(8,128)(2,1)}), bf16[3,64,128,128]{3,2,0,1:T(8,128)(2,1)}, u32[]{:S(2)}, u32[]{:S(2)}) async-start(bf16[3,64,128,128]{3,2,0,1:T(8,128)(2,1)} %select_bitcast_fusion), calls=%async_computation | async-start | bytes 12582912 | tf_op jit(solution)/shard_map/all_to_all | solution.py:39
  49.2 124.3 %reduce-scatter.2.cloned.1.call-start = ((), (), s32[]{:S(2)}) async-start(), calls=%async_computation.4 | async-start | bytes 1769472 | tf_op jit(solution)/shard_map/reduce_scatter | solution.py:48
  49.3 4.3 %copy-start.1 = (s32[24,1]{0,1:T(1,128)S(1)}, s32[24,1]{0,1:T(1,128)}, u32[]{:S(2)}) copy-start(s32[24,1]{0,1:T(1,128)} %param.10) | copy-start | bytes 292
Sparse Core Ops, SparseCore 0:
  134.2 39.2 reduce-scatter.1

commit v2 on v1

v2 whole, which is shorter than its diff:
```python
import jax
import jax.numpy as jnp
from jax import lax
from jax.experimental import pallas as pl
from jax.experimental.pallas import tpu as pltpu
from jax.sharding import PartitionSpec as P

MESH = pl.DeviceIdType.MESH
CHIPS = (
    (0, 0), (0, 1), (1, 0), (0, 3),
    (3, 0), (1, 1), (3, 3), (1, 3),
    (3, 1), (2, 0), (0, 2), (2, 1),
    (1, 2), (2, 3), (3, 2), (2, 2),
)
WINDOW = 4
CHUNKS = len(CHIPS)
F32 = jnp.float32
BF16 = jnp.bfloat16


def flip(value, bits):
    high, low = value // 2, value % 2
    return ((high + bits // 2) % 2) * 2 + (low + bits % 2) % 2


def kernel(
    trial, left, right, lslot, dest, rslot, out,
    tv, lv, rv, xb, sendb, recvb, part, ring, total, crossed,
    ktab, rtab, itab, ktab_s, itab_s,
    load_sem, tab_sem, isend, irecv, rsend, rrecv, gsend, grecv, csend, crecv, zsend, zrecv,
):
    me = lax.axis_index("sec")
    z = lax.axis_index("mpo")
    core, x, y = me % 2, (me // 2) % 4, me // 8
    depth = 1 - 2 * core
    planes = 8

    def partner(chunk, i):
        dy, dx = CHIPS[chunk]
        return flip(y, dy) * 8 + flip(x, dx) * 2 + (core + i) % 2

    everyone = [(t, i) for t in range(CHUNKS) for i in range(2) if (t, i) != (0, 0)]

    barrier = pltpu.get_barrier_semaphore()
    for t, i in everyone:
        pl.semaphore_signal(
            barrier, inc=1, device_id={"sec": partner(t, i)}, device_id_type=MESH
        )
    for step in range(1, planes):
        pl.semaphore_signal(
            barrier, inc=1, device_id={"mpo": (z + step) % planes}, device_id_type=MESH
        )
    loads = [
        pltpu.make_async_copy(right, rv, load_sem.at[0]),
        pltpu.make_async_copy(trial, tv, load_sem.at[1]),
        pltpu.make_async_copy(left, lv, load_sem.at[2]),
    ]
    for load in loads:
        load.start()

    lane = lax.broadcasted_iota(jnp.int32, (1, 128), 1)
    seen = jnp.zeros((1, 128), jnp.int32)
    first_k = jnp.full((1, 128), -1, jnp.int32)
    second_k = jnp.full((1, 128), -1, jnp.int32)
    first_r = jnp.zeros((1, 128), jnp.int32)
    second_r = jnp.zeros((1, 128), jnp.int32)
    for k in range(24):
        hit = lane == dest[k, 0]
        is_first = hit & (seen == 0)
        is_second = hit & (seen == 1)
        first_k = jnp.where(is_first, k, first_k)
        second_k = jnp.where(is_second, k, second_k)
        first_r = jnp.where(is_first, rslot[k], first_r)
        second_r = jnp.where(is_second, rslot[k], second_r)
        seen = seen + hit.astype(jnp.int32)
    ktab[0:1, :] = first_k
    ktab[1:2, :] = second_k
    rtab[0:1, :] = first_r
    rtab[1:2, :] = second_r
    to_smem = pltpu.make_async_copy(ktab, ktab_s, tab_sem.at[0])
    to_smem.start()
    to_smem.wait()

    pl.semaphore_wait(barrier, len(everyone) + planes - 1)

    asks = []
    for t, i in everyone:
        o = 2 * t + i
        asks.append(
            pltpu.make_async_remote_copy(
                src_ref=rtab, dst_ref=itab.at[o], send_sem=isend.at[o], recv_sem=irecv.at[o],
                device_id={"sec": partner(t, i)}, device_id_type=MESH,
            )
        )
        asks[-1].start()
    itab[0] = rtab[...]
    loads[0].wait()
    for ask in asks:
        ask.wait_recv()
    asked = pltpu.make_async_copy(itab, itab_s, tab_sem.at[1])
    asked.start()
    asked.wait()

    def whole(t, i):
        o = 2 * t + i
        return pltpu.make_async_remote_copy(
            src_ref=sendb.at[o], dst_ref=recvb.at[o], send_sem=rsend.at[o], recv_sem=rrecv.at[o],
            device_id={"sec": partner(t, i)}, device_id_type=MESH,
        )

    def send_window(start):
        group = [(t, i) for t in range(start, start + WINDOW) for i in range(2)]
        for c in range(2):
            for t, i in group:
                o = 2 * t + i
                slot = itab_s[o, c, me]
                for b in range(3):
                    if o == 0:
                        recvb[0, c, b] = rv[b, slot]
                    else:
                        sendb[o, c, b] = rv[b, slot]
            for b in range(3):
                for t, i in group:
                    o = 2 * t + i
                    if o:
                        pltpu.make_async_remote_copy(
                            src_ref=sendb.at[o, c, b], dst_ref=recvb.at[o, c, b],
                            send_sem=rsend.at[o], recv_sem=rrecv.at[o],
                            device_id={"sec": partner(t, i)}, device_id_type=MESH,
                        ).start()

    def left_products():
        def body(k, carry):
            a = lslot[k]
            stacked = jnp.concatenate([lv[b, a] for b in range(3)], axis=0)
            vectors = jnp.concatenate([tv[0, k], tv[1, k]], axis=1)
            product = jnp.dot(stacked, vectors, preferred_element_type=F32).astype(BF16)
            for b in range(3):
                for v in range(2):
                    xb[k, b, v * 128 : (v + 1) * 128, :] = product[
                        b * 128 : (b + 1) * 128, v * 128 : (v + 1) * 128
                    ]
            return carry

        lax.fori_loop(0, 24, body, 0)

    def right_products(t):
        for i in range(2):
            if (t, i) != (0, 0):
                whole(t, i).wait_recv()

        def body(q, carry):
            i, c = q // 2, q % 2
            k = ktab_s[c, partner(t, i)]
            at = jnp.maximum(k, 0)
            o = 2 * t + i
            xs = jnp.concatenate([xb[at, b] for b in range(3)], axis=1)
            rs = jnp.concatenate([recvb[o, c, b] for b in range(3)], axis=1)
            value = lax.dot_general(xs, rs, (((1,), (1,)), ((), ())), preferred_element_type=F32)
            value = jnp.where(k >= 0, value, 0.0).astype(BF16)
            for v in range(2):
                for p in range(planes):
                    row = v * 128 + p * 16
                    part[t, p, q * 2 + v] = value[row : row + 16]
            return carry

        lax.fori_loop(0, 4, body, 0)

    def hop(t, slot):
        if slot < 4:
            piece = (z + planes + (slot - 4) * depth) % planes
            to = (z + planes - depth) % planes
        else:
            piece = (z + planes + (7 - slot) * depth) % planes
            to = (z + planes + depth) % planes
        return pltpu.make_async_remote_copy(
            src_ref=part.at[t, piece], dst_ref=ring.at[t, slot],
            send_sem=gsend.at[t, slot], recv_sem=grecv.at[t, slot],
            device_id={"mpo": to}, device_id_type=MESH,
        )

    def add_in(t, slot):
        hop(t, slot - 1).wait_recv()
        if slot < 4:
            piece = (z + planes + (slot - 4) * depth) % planes
        else:
            piece = (z + planes + (7 - slot) * depth) % planes
        part[t, piece] = (part[t, piece].astype(F32) + ring[t, slot - 1].astype(F32)).astype(BF16)

    def ring_step(t, step):
        if step:
            add_in(t, step)
        hop(t, step).start()
        if step < 3:
            if step:
                add_in(t, 4 + step)
            hop(t, 4 + step).start()

    def across(t, i):
        o = 2 * t + i
        return pltpu.make_async_remote_copy(
            src_ref=total.at[t, pl.ds(4 * i, 4)], dst_ref=crossed.at[o],
            send_sem=csend.at[o], recv_sem=crecv.at[o],
            device_id={"sec": partner(t, i)}, device_id_type=MESH,
        )

    def finish_sum(t):
        hop(t, 3).wait_recv()
        hop(t, 6).wait_recv()
        done = (
            part[t, z].astype(F32) + ring[t, 3].astype(F32) + ring[t, 6].astype(F32)
        ).astype(BF16)
        total[t] = done
        for i in range(2):
            if (t, i) == (0, 0):
                crossed[0] = done[0:4]
            else:
                across(t, i).start()

    def place(t, i):
        source = partner(t, i)
        to, w = source // 4, source % 4
        src = crossed.at[2 * t + i]
        return to, pltpu.make_async_remote_copy(
            src_ref=src, dst_ref=out.at[pl.ds(4 * w, 4), pl.ds(16 * z, 16)],
            send_sem=zsend.at[2 * t + i], recv_sem=zrecv.at[w, z],
            device_id={"mpo": to}, device_id_type=MESH,
        ), pltpu.make_async_copy(
            src, out.at[pl.ds(4 * w, 4), pl.ds(16 * z, 16)], zrecv.at[w, z]
        )

    def place_rows(t):
        for i in range(2):
            if (t, i) != (0, 0):
                across(t, i).wait_recv()
            to, remote, own = place(t, i)

            @pl.when(to == z)
            def _():
                own.start()

            @pl.when(to != z)
            def _():
                remote.start()

    send_window(0)
    send_window(WINDOW)
    loads[1].wait()
    loads[2].wait()
    left_products()
    for turn in range(CHUNKS + 5):
        if 0 <= turn - 5 < CHUNKS:
            place_rows(turn - 5)
        if 0 <= turn - 4 < CHUNKS:
            finish_sum(turn - 4)
        for step in (3, 2, 1):
            if 0 <= turn - step < CHUNKS:
                ring_step(turn - step, step)
        if turn < CHUNKS:
            if turn % WINDOW == 0 and turn + 2 * WINDOW < CHUNKS:
                send_window(turn + 2 * WINDOW)
            right_products(turn)
            ring_step(turn, 0)

    for ask in asks:
        ask.wait_send()
    for t, i in everyone:
        whole(t, i).wait_send()
        across(t, i).wait_send()
    for t in range(CHUNKS):
        for slot in range(7):
            hop(t, slot).wait_send()
        for i in range(2):
            to, remote, own = place(t, i)

            @pl.when(to != z)
            def _():
                remote.wait_send()
    for w in range(4):
        for p in range(planes):
            pltpu.make_async_copy(
                crossed.at[0], out.at[pl.ds(4 * w, 4), pl.ds(16 * p, 16)], zrecv.at[w, p]
            ).wait()


def local(trial, left_env, right_env, left_slot, dest, right_slot):
    anywhere = pl.BlockSpec(memory_space=pl.ANY)
    scalars = pl.BlockSpec(memory_space=pltpu.SMEM)
    dma = pltpu.SemaphoreType.DMA
    rows = pl.pallas_call(
        kernel,
        out_shape=jax.ShapeDtypeStruct((16, 128, 128), BF16),
        in_specs=[anywhere] * 3 + [scalars] * 3,
        out_specs=anywhere,
        scratch_shapes=[
            pltpu.VMEM((2, 24, 128, 128), BF16),
            pltpu.VMEM((3, 32, 128, 128), BF16),
            pltpu.VMEM((3, 32, 128, 128), BF16),
            pltpu.VMEM((24, 3, 256, 128), BF16),
            pltpu.VMEM((32, 2, 3, 128, 128), BF16),
            pltpu.VMEM((32, 2, 3, 128, 128), BF16),
            pltpu.VMEM((CHUNKS, 8, 8, 16, 128), BF16),
            pltpu.VMEM((CHUNKS, 7, 8, 16, 128), BF16),
            pltpu.VMEM((CHUNKS, 8, 16, 128), BF16),
            pltpu.VMEM((32, 4, 16, 128), BF16),
            pltpu.VMEM((2, 128), jnp.int32),
            pltpu.VMEM((2, 128), jnp.int32),
            pltpu.VMEM((32, 2, 128), jnp.int32),
            pltpu.SMEM((2, 128), jnp.int32),
            pltpu.SMEM((32, 2, 128), jnp.int32),
            dma((3,)),
            dma((2,)),
            dma((32,)),
            dma((32,)),
            dma((32,)),
            dma((32,)),
            dma((CHUNKS, 7)),
            dma((CHUNKS, 7)),
            dma((32,)),
            dma((32,)),
            dma((32,)),
            dma((4, 8)),
        ],
        compiler_params=pltpu.CompilerParams(
            collective_id=0, has_side_effects=True, vmem_limit_bytes=50 * 1024 * 1024
        ),
        name="products",
    )(trial, left_env, right_env, left_slot, dest, right_slot)
    return rows.reshape(8, 2, 128, 128)


def solution(mesh):
    placed = (
        P(None, "sec", None, None),
        P("mpo", "sec", None, None),
        P("mpo", "sec", None, None),
        P("sec"),
        P("sec", None),
        P("sec"),
    )
    return jax.shard_map(
        local,
        mesh=mesh,
        in_specs=placed,
        out_specs=P(("sec", "mpo"), None, None, None),
        check_vma=False,
    )
```

time: 228 us -> 173 us (0.76)
  Pallas kernels: 0 us -> 167 us
  waiting for transfers between devices: 108 us -> 0 us
  blocking collectives: 69.1 us -> 0 us
  between operations: 13.5 us -> 0.01 us
  local copies, waits for them, and re-layouts: 17.1 us -> 4.25 us
  other arithmetic: 8.82 us -> 0 us
  matrix products: 6.74 us -> 0 us
  starting transfers between devices: 5.13 us -> 0 us
    pallas_call x0 -> x1, Pallas kernels: none -> 167 us  [local(): pl.pallas_call(kernel, out_shape=jax.ShapeDtypeStruct((16, 128, 128), BF1...]
    all_to_all x1 -> x0, waiting for transfers between devices: 68.4 us -> none  [local(): lax.all_to_all(outgoing, 'sec', split_axis=1, concat_axis=1, tiled=True)]
    all_to_all x2 -> x0, blocking collectives: 43.2 us -> none  [the longest x1 22.9 us: local(): lax.all_to_all(placed, 'sec', split_axis=0, concat_axis=0, tiled=True)]
    reduce_scatter x1 -> x0, waiting for transfers between devices: 39.2 us -> none  [local(): summed = lax.psum_scatter(partials, 'mpo', scatter_dimension=2, tiled=True)]
    all_gather x1 -> x0, blocking collectives: 25.9 us -> none  [local(): lax.all_gather(jnp.stack([targets, right_slot]), 'sec', axis=0, tiled=False)]
    gather x4 -> x0, local copies, waits for them, and re-layouts: 15.7 us -> none  [the longest x1 5.13 us: local(): right_blocks = jnp.take(incoming, positions, axis=1)]
    select_n x5 -> x0, other arithmetic: 7.36 us -> none  [the longest x2 6.11 us: local(): outgoing = jnp.take(right_env, asked, axis=1)]
    dot_general x1 -> x0, matrix products: 6.74 us -> none  [local(): jnp.einsum('bvkil,bkml->kvim', products, right_blocks, preferred_element_...]
  transfers between devices with their start and end apart: 2 -> 0, of which waited for: 2 -> 0; matrix products, arithmetic and copies ran while one was open for 2% -> 0% of each run, Pallas kernels for 0% -> 0%
where the time goes in v2:
time: 173 us; the launch traced here: 172 us
  Pallas kernels  167 us (97%)
  local copies, waits for them, and re-layouts  4.25 us (2%)
    pallas_call x1, Pallas kernels, local(): pl.pallas_call(kernel, out_shape=jax.ShapeDtypeStruct((16, 128, 128), BF1...  167 us
    unnamed x8, local copies, waits for them, and re-layouts  4.25 us

profile of v2, /device:TPU:1, one launch (start us, length us, event | category | flops | bytes accessed | tf_op | source)
XLA Modules:
  0.0 171.6 jit_solution(16792547310075524302)
XLA Ops:
  0.0 0.7 copy.7.dest
  0.7 0.0 copy-start
  0.7 1.4 copy-done
  2.1 0.0 copy-start.1
  2.1 0.7 copy-done.1
  2.8 0.0 copy-start.2
  2.8 0.7 copy-done.2
  3.5 167.3 %products.1 = bf16[16,128,128]{2,1,0:T(8,128)(2,1)S(1)} custom-call(bf16[2,24,128,128]{3,2,1,0:T(8,128)(2,1)S(1)} %copy-done, bf16[3,32,128,128]{3,2,1,0:T(8,128)(2,1)} %left.1, bf16[3,32,128,128]{3,2,1,0:T(8,128)(2,1)} %right.1, s32[24]{0:T(128)S(1)} %copy-done.1, s32[24,1]{1,0:T(8,128)S(1)} %copy.7.dest, s32[24]{0:T(128)S(1)} %copy-done.2), custom_call_target="tpu_custom_call" | custom-call | tf_op jit(solution)/shard_map/products/pallas_call | solution.py:290
  170.8 0.8 copy.9
Async XLA Ops:
  0.7 1.4 copy-start
  2.1 0.7 copy-start.1
  2.8 0.7 copy-start.2

commit v3 on v2

v3 whole, which is shorter than its diff:
```python
import jax
import jax.numpy as jnp
from jax import lax
from jax.experimental import pallas as pl
from jax.experimental.pallas import tpu as pltpu
from jax.sharding import PartitionSpec as P

MESH = pl.DeviceIdType.MESH
CHIPS = (
    (0, 0), (0, 1), (1, 0), (0, 3),
    (3, 0), (1, 1), (3, 3), (1, 3),
    (3, 1), (2, 0), (0, 2), (2, 1),
    (1, 2), (2, 3), (3, 2), (2, 2),
)
AHEAD = 6
SLACK = 3
CHUNKS = len(CHIPS)
F32 = jnp.float32
BF16 = jnp.bfloat16


def flip(value, bits):
    high, low = value // 2, value % 2
    return ((high + bits // 2) % 2) * 2 + (low + bits % 2) % 2


def kernel(
    trial, left, right, lslot_hbm, dest_hbm, rslot_hbm, out,
    tv, lv, rv, xb, sendb, recvb, part, ring, total, crossed,
    ktab, rtab, itab, ktab_s, itab_s, lslot, dest, rslot,
    load_sem, small_sem, tab_sem, isend, irecv, rsend, rrecv, gsend, grecv, csend, crecv, zsend, zrecv,
):
    me = lax.axis_index("sec")
    z = lax.axis_index("mpo")
    core, x, y = me % 2, (me // 2) % 4, me // 8
    depth = 1 - 2 * core
    planes = 8

    def partner(chunk, i):
        dy, dx = CHIPS[chunk]
        return flip(y, dy) * 8 + flip(x, dx) * 2 + (core + i) % 2

    everyone = [(t, i) for t in range(CHUNKS) for i in range(2) if (t, i) != (0, 0)]

    smalls = [
        pltpu.make_async_copy(dest_hbm, dest, small_sem.at[0]),
        pltpu.make_async_copy(rslot_hbm, rslot, small_sem.at[1]),
        pltpu.make_async_copy(lslot_hbm, lslot, small_sem.at[2]),
    ]
    for small in smalls:
        small.start()

    barrier = pltpu.get_barrier_semaphore()
    for t, i in everyone:
        pl.semaphore_signal(
            barrier, inc=1, device_id={"sec": partner(t, i)}, device_id_type=MESH
        )
    for step in range(1, planes):
        pl.semaphore_signal(
            barrier, inc=1, device_id={"mpo": (z + step) % planes}, device_id_type=MESH
        )
    loads = [
        pltpu.make_async_copy(right, rv, load_sem.at[0]),
        pltpu.make_async_copy(trial, tv, load_sem.at[1]),
        pltpu.make_async_copy(left, lv, load_sem.at[2]),
    ]
    for load in loads:
        load.start()

    for small in smalls:
        small.wait()

    lane = lax.broadcasted_iota(jnp.int32, (1, 128), 1)
    seen = jnp.zeros((1, 128), jnp.int32)
    first_k = jnp.full((1, 128), -1, jnp.int32)
    second_k = jnp.full((1, 128), -1, jnp.int32)
    first_r = jnp.zeros((1, 128), jnp.int32)
    second_r = jnp.zeros((1, 128), jnp.int32)
    for k in range(24):
        hit = lane == dest[k, 0]
        is_first = hit & (seen == 0)
        is_second = hit & (seen == 1)
        first_k = jnp.where(is_first, k, first_k)
        second_k = jnp.where(is_second, k, second_k)
        first_r = jnp.where(is_first, rslot[k], first_r)
        second_r = jnp.where(is_second, rslot[k], second_r)
        seen = seen + hit.astype(jnp.int32)
    ktab[0:1, :] = first_k
    ktab[1:2, :] = second_k
    rtab[0:1, :] = first_r
    rtab[1:2, :] = second_r
    to_smem = pltpu.make_async_copy(ktab, ktab_s, tab_sem.at[0])
    to_smem.start()
    to_smem.wait()

    pl.semaphore_wait(barrier, len(everyone) + planes - 1)

    for t, i in everyone:
        o = 2 * t + i
        pltpu.make_async_remote_copy(
            src_ref=rtab, dst_ref=itab.at[o], send_sem=isend, recv_sem=irecv,
            device_id={"sec": partner(t, i)}, device_id_type=MESH,
        ).start()
    itab[0] = rtab[...]
    loads[0].wait()
    all_asks = pltpu.make_async_copy(itab.at[pl.ds(1, 31)], itab.at[pl.ds(1, 31)], irecv)
    all_asks.wait()
    asked = pltpu.make_async_copy(itab, itab_s, tab_sem.at[1])
    asked.start()
    asked.wait()

    def send_chunk(t):
        for c in range(2):
            for i in range(2):
                o = 2 * t + i
                slot = itab_s[o, c, me]
                for b in range(3):
                    if o == 0:
                        recvb[0, c, b] = rv[b, slot]
                    else:
                        sendb[o, c, b] = rv[b, slot]
            for b in range(3):
                for i in range(2):
                    o = 2 * t + i
                    if o:
                        pltpu.make_async_remote_copy(
                            src_ref=sendb.at[o, c, b], dst_ref=recvb.at[o, c, b],
                            send_sem=rsend, recv_sem=rrecv.at[t],
                            device_id={"sec": partner(t, i)}, device_id_type=MESH,
                        ).start()

    def left_products():
        def body(k, carry):
            a = lslot[k]
            stacked = jnp.concatenate([lv[b, a] for b in range(3)], axis=0)
            vectors = jnp.concatenate([tv[0, k], tv[1, k]], axis=1)
            product = jnp.dot(stacked, vectors, preferred_element_type=F32).astype(BF16)
            for b in range(3):
                for v in range(2):
                    xb[k, b, v * 128 : (v + 1) * 128, :] = product[
                        b * 128 : (b + 1) * 128, v * 128 : (v + 1) * 128
                    ]
            return carry

        lax.fori_loop(0, 24, body, 0)

    def right_products(t):
        landed = recvb.at[pl.ds(2 * t, 2)] if t else recvb.at[1]
        pltpu.make_async_copy(landed, landed, rrecv.at[t]).wait()

        def body(q, carry):
            i, c = q // 2, q % 2
            k = ktab_s[c, partner(t, i)]
            at = jnp.maximum(k, 0)
            o = 2 * t + i
            xs = jnp.concatenate([xb[at, b] for b in range(3)], axis=1)
            rs = jnp.concatenate([recvb[o, c, b] for b in range(3)], axis=1)
            value = lax.dot_general(xs, rs, (((1,), (1,)), ((), ())), preferred_element_type=F32)
            value = jnp.where(k >= 0, value, 0.0).astype(BF16)
            for v in range(2):
                for p in range(planes):
                    row = v * 128 + p * 16
                    part[t, p, q * 2 + v] = value[row : row + 16]
            return carry

        lax.fori_loop(0, 4, body, 0)

    def hop(t, step, way):
        back = 4 - step if way == 0 else step - 3
        piece = (z + planes - back * depth) % planes
        to = (z + planes + (depth if way else -depth)) % planes
        return piece, pltpu.make_async_remote_copy(
            src_ref=part.at[t, piece], dst_ref=ring.at[t, step, way],
            send_sem=gsend, recv_sem=grecv.at[t, step],
            device_id={"mpo": to}, device_id_type=MESH,
        )

    def ring_step(t, step):
        ways = range(2 if step < 3 else 1)
        if step:
            landed = ring.at[t, step - 1]
            pltpu.make_async_copy(landed, landed, grecv.at[t, step - 1]).wait()
        for way in ways:
            piece, copy = hop(t, step, way)
            if step:
                part[t, piece] = (
                    part[t, piece].astype(F32) + ring[t, step - 1, way].astype(F32)
                ).astype(BF16)
            copy.start()

    def across(t, i):
        o = 2 * t + i
        return pltpu.make_async_remote_copy(
            src_ref=total.at[t, pl.ds(4 * i, 4)], dst_ref=crossed.at[o],
            send_sem=csend, recv_sem=crecv.at[t],
            device_id={"sec": partner(t, i)}, device_id_type=MESH,
        )

    def finish_sum(t):
        pltpu.make_async_copy(ring.at[t, 3, 0], ring.at[t, 3, 0], grecv.at[t, 3]).wait()
        done = (
            part[t, z].astype(F32) + ring[t, 3, 0].astype(F32) + ring[t, 2, 1].astype(F32)
        ).astype(BF16)
        total[t] = done
        for i in range(2):
            if (t, i) == (0, 0):
                crossed[0] = done[0:4]
            else:
                across(t, i).start()

    def place(t, i):
        source = partner(t, i)
        to, w = source // 4, source % 4
        src = crossed.at[2 * t + i]
        return to, pltpu.make_async_remote_copy(
            src_ref=src, dst_ref=out.at[pl.ds(4 * w, 4), pl.ds(16 * z, 16)],
            send_sem=zsend, recv_sem=zrecv,
            device_id={"mpo": to}, device_id_type=MESH,
        ), pltpu.make_async_copy(
            src, out.at[pl.ds(4 * w, 4), pl.ds(16 * z, 16)], zrecv
        )

    def place_rows(t):
        landed = crossed.at[pl.ds(2 * t, 2)] if t else crossed.at[1]
        pltpu.make_async_copy(landed, landed, crecv.at[t]).wait()
        for i in range(2):
            to, remote, own = place(t, i)

            @pl.when(to == z)
            def _():
                own.start()

            @pl.when(to != z)
            def _():
                remote.start()

    for t in range(AHEAD):
        send_chunk(t)
    loads[1].wait()
    loads[2].wait()
    left_products()
    for turn in range(CHUNKS + 5 * SLACK):
        if 0 <= turn - 5 * SLACK < CHUNKS:
            place_rows(turn - 5 * SLACK)
        if 0 <= turn - 4 * SLACK < CHUNKS:
            finish_sum(turn - 4 * SLACK)
        for step in (3, 2, 1):
            if 0 <= turn - step * SLACK < CHUNKS:
                ring_step(turn - step * SLACK, step)
        if turn < CHUNKS:
            if turn + AHEAD < CHUNKS:
                send_chunk(turn + AHEAD)
            right_products(turn)
            ring_step(turn, 0)

    for sent, sem in (
        (itab.at[pl.ds(1, 31)], isend),
        (sendb.at[pl.ds(1, 31)], rsend),
        (part.at[:, pl.ds(0, 7)], gsend),
        (crossed.at[pl.ds(1, 31)], csend),
        (crossed.at[pl.ds(0, 28)], zsend),
        (out, zrecv),
    ):
        pltpu.make_async_copy(sent, sent, sem).wait()


def local(trial, left_env, right_env, left_slot, dest, right_slot):
    anywhere = pl.BlockSpec(memory_space=pl.ANY)
    dma = pltpu.SemaphoreType.DMA
    rows = pl.pallas_call(
        kernel,
        out_shape=jax.ShapeDtypeStruct((16, 128, 128), BF16),
        in_specs=[anywhere] * 6,
        out_specs=anywhere,
        scratch_shapes=[
            pltpu.VMEM((2, 24, 128, 128), BF16),
            pltpu.VMEM((3, 32, 128, 128), BF16),
            pltpu.VMEM((3, 32, 128, 128), BF16),
            pltpu.VMEM((24, 3, 256, 128), BF16),
            pltpu.VMEM((32, 2, 3, 128, 128), BF16),
            pltpu.VMEM((32, 2, 3, 128, 128), BF16),
            pltpu.VMEM((CHUNKS, 8, 8, 16, 128), BF16),
            pltpu.VMEM((CHUNKS, 4, 2, 8, 16, 128), BF16),
            pltpu.VMEM((CHUNKS, 8, 16, 128), BF16),
            pltpu.VMEM((32, 4, 16, 128), BF16),
            pltpu.VMEM((2, 128), jnp.int32),
            pltpu.VMEM((2, 128), jnp.int32),
            pltpu.VMEM((32, 2, 128), jnp.int32),
            pltpu.SMEM((2, 128), jnp.int32),
            pltpu.SMEM((32, 2, 128), jnp.int32),
            pltpu.SMEM((24,), jnp.int32),
            pltpu.SMEM((24, 1), jnp.int32),
            pltpu.SMEM((24,), jnp.int32),
            dma((3,)),
            dma((3,)),
            dma((2,)),
            dma,
            dma,
            dma,
            dma((CHUNKS,)),
            dma,
            dma((CHUNKS, 4)),
            dma,
            dma((CHUNKS,)),
            dma,
            dma,
        ],
        compiler_params=pltpu.CompilerParams(
            collective_id=0, has_side_effects=True, vmem_limit_bytes=60 * 1024 * 1024
        ),
        name="products",
    )(trial, left_env, right_env, left_slot, dest, right_slot)
    return rows.reshape(8, 2, 128, 128)


def solution(mesh):
    placed = (
        P(None, "sec", None, None),
        P("mpo", "sec", None, None),
        P("mpo", "sec", None, None),
        P("sec"),
        P("sec", None),
        P("sec"),
    )
    return jax.shard_map(
        local,
        mesh=mesh,
        in_specs=placed,
        out_specs=P(("sec", "mpo"), None, None, None),
        check_vma=False,
    )
```

time: 173 us -> 134 us (0.77)
  Pallas kernels: 167 us -> 128 us
    pallas_call x1, Pallas kernels: 167 us -> 128 us  [local(): pl.pallas_call(kernel, out_shape=jax.ShapeDtypeStruct((16, 128, 128), BF1...]
    unnamed x8 -> x2, local copies, waits for them, and re-layouts: 4.25 us -> 3.22 us
where the time goes in v3:
time: 134 us; the launch traced here: 132 us
  Pallas kernels  128 us (96%)
  local copies, waits for them, and re-layouts  3.22 us (2%)
    pallas_call x1, Pallas kernels, local(): pl.pallas_call(kernel, out_shape=jax.ShapeDtypeStruct((16, 128, 128), BF1...  128 us
    unnamed x2, local copies, waits for them, and re-layouts  3.22 us

profile of v3, /device:TPU:1, one launch (start us, length us, event | category | flops | bytes accessed | tf_op | source)
XLA Modules:
  0.0 131.5 jit_solution(10117323123228765104)
XLA Ops:
  0.0 1.3 %copy.7.dest_hbm = s32[24,1]{1,0:T(8,128)} copy(s32[24,1]{0,1:T(1,128)} %param.10) | data formatting | bytes 192 | tf_op args[4]
  1.3 128.3 %products.1 = bf16[16,128,128]{2,1,0:T(8,128)(2,1)} custom-call(bf16[2,24,128,128]{3,2,1,0:T(8,128)(2,1)} %trial.1, bf16[3,32,128,128]{3,2,1,0:T(8,128)(2,1)} %left.1, bf16[3,32,128,128]{3,2,1,0:T(8,128)(2,1)} %right.1, s32[24]{0:T(128)} %lslot_hbm.1, s32[24,1]{1,0:T(8,128)} %copy.7.dest_hbm, s32[24]{0:T(128)} %rslot_hbm.1), custom_call_target="tpu_custom_call" | custom-call | tf_op jit(solution)/shard_map/products/pallas_call | solution.py:270
  129.6 1.9 %copy.9 = bf16[8,2,128,128]{3,2,1,0:T(8,128)(2,1)} copy(bf16[8,2,128,128]{3,2,1,0:T(8,128)(2,1)} %bitcast.1) | data formatting | bytes 1048576

commit v4 on v3

--- a/solution.py
+++ b/solution.py
@@ -13,7 +13,7 @@
     (1, 2), (2, 3), (3, 2), (2, 2),
 )
 AHEAD = 6
-SLACK = 3
+LAGS = (0, 2, 4, 6, 8, 12)
 CHUNKS = len(CHIPS)
 F32 = jnp.float32
 BF16 = jnp.bfloat16
@@ -239,14 +239,14 @@
     loads[1].wait()
     loads[2].wait()
     left_products()
-    for turn in range(CHUNKS + 5 * SLACK):
-        if 0 <= turn - 5 * SLACK < CHUNKS:
-            place_rows(turn - 5 * SLACK)
-        if 0 <= turn - 4 * SLACK < CHUNKS:
-            finish_sum(turn - 4 * SLACK)
+    for turn in range(CHUNKS + LAGS[5]):
+        if 0 <= turn - LAGS[5] < CHUNKS:
+            place_rows(turn - LAGS[5])
+        if 0 <= turn - LAGS[4] < CHUNKS:
+            finish_sum(turn - LAGS[4])
         for step in (3, 2, 1):
-            if 0 <= turn - step * SLACK < CHUNKS:
-                ring_step(turn - step * SLACK, step)
+            if 0 <= turn - LAGS[step] < CHUNKS:
+                ring_step(turn - LAGS[step], step)
         if turn < CHUNKS:
             if turn + AHEAD < CHUNKS:
                 send_chunk(turn + AHEAD)

time: 134 us -> 130 us (0.970); the launches traced: 132 us -> 129 us
  Pallas kernels: 128 us -> 126 us
    pallas_call x1, Pallas kernels: 128 us -> 126 us  [local(): pl.pallas_call(kernel, out_shape=jax.ShapeDtypeStruct((16, 128, 128), BF1...]
where the time goes in v4:
time: 130 us; the launch traced here: 129 us
  Pallas kernels  126 us (97%)
  local copies, waits for them, and re-layouts  3.22 us (2%)
    pallas_call x1, Pallas kernels, local(): pl.pallas_call(kernel, out_shape=jax.ShapeDtypeStruct((16, 128, 128), BF1...  126 us
    unnamed x2, local copies, waits for them, and re-layouts  3.22 us

profile of v4, /device:TPU:1, one launch (start us, length us, event | category | flops | bytes accessed | tf_op | source)
XLA Modules:
  0.0 129.0 jit_solution(2254592498621880763)
XLA Ops:
  0.0 1.3 %copy.7.dest_hbm = s32[24,1]{1,0:T(8,128)} copy(s32[24,1]{0,1:T(1,128)} %param.10) | data formatting | bytes 192 | tf_op args[4]
  1.3 125.8 %products.1 = bf16[16,128,128]{2,1,0:T(8,128)(2,1)} custom-call(bf16[2,24,128,128]{3,2,1,0:T(8,128)(2,1)} %trial.1, bf16[3,32,128,128]{3,2,1,0:T(8,128)(2,1)} %left.1, bf16[3,32,128,128]{3,2,1,0:T(8,128)(2,1)} %right.1, s32[24]{0:T(128)} %lslot_hbm.1, s32[24,1]{1,0:T(8,128)} %copy.7.dest_hbm, s32[24]{0:T(128)} %rslot_hbm.1), custom_call_target="tpu_custom_call" | custom-call | tf_op jit(solution)/shard_map/products/pallas_call | solution.py:270
  127.2 1.9 %copy.9 = bf16[8,2,128,128]{3,2,1,0:T(8,128)(2,1)} copy(bf16[8,2,128,128]{3,2,1,0:T(8,128)(2,1)} %bitcast.1) | data formatting | bytes 1048576

commit v5 on v4

--- a/solution.py
+++ b/solution.py
@@ -13,7 +13,7 @@
     (1, 2), (2, 3), (3, 2), (2, 2),
 )
 AHEAD = 6
-LAGS = (0, 2, 4, 6, 8, 12)
+LAGS = (0, 2, 4, 6, 8, 13)
 CHUNKS = len(CHIPS)
 F32 = jnp.float32
 BF16 = jnp.bfloat16

time: 130 us -> 130 us (level)
  no operation moved by 1% of the time
where the time goes in v5:
time: 130 us; the launch traced here: 128 us
  Pallas kernels  125 us (96%)
  local copies, waits for them, and re-layouts  3.22 us (2%)
    pallas_call x1, Pallas kernels, local(): pl.pallas_call(kernel, out_shape=jax.ShapeDtypeStruct((16, 128, 128), BF1...  125 us
    unnamed x2, local copies, waits for them, and re-layouts  3.22 us

profile of v5, /device:TPU:1, one launch (start us, length us, event | category | flops | bytes accessed | tf_op | source)
XLA Modules:
  0.0 128.4 jit_solution(13149637627252514230)
XLA Ops:
  0.0 1.3 %copy.7.dest_hbm = s32[24,1]{1,0:T(8,128)} copy(s32[24,1]{0,1:T(1,128)} %param.10) | data formatting | bytes 192 | tf_op args[4]
  1.3 125.2 %products.1 = bf16[16,128,128]{2,1,0:T(8,128)(2,1)} custom-call(bf16[2,24,128,128]{3,2,1,0:T(8,128)(2,1)} %trial.1, bf16[3,32,128,128]{3,2,1,0:T(8,128)(2,1)} %left.1, bf16[3,32,128,128]{3,2,1,0:T(8,128)(2,1)} %right.1, s32[24]{0:T(128)} %lslot_hbm.1, s32[24,1]{1,0:T(8,128)} %copy.7.dest_hbm, s32[24]{0:T(128)} %rslot_hbm.1), custom_call_target="tpu_custom_call" | custom-call | tf_op jit(solution)/shard_map/products/pallas_call | solution.py:270
  126.5 1.9 %copy.9 = bf16[8,2,128,128]{3,2,1,0:T(8,128)(2,1)} copy(bf16[8,2,128,128]{3,2,1,0:T(8,128)(2,1)} %bitcast.1) | data formatting | bytes 1048576
